TPU v7x, 32 devices: a whole 2x2x4 slice. The times are simulated.
32 devices in a mesh: dom: 8 (over z, x), row: 4 (over y, core).
Axes of the slice: x: 2, y: 2, z: 4, core: 2. Of those that a mesh axis runs over, the one named last changes fastest.
Arguments:
- right_side: float32 [8192, 128], P(('dom', 'row')), may hold values from -6 to 6
- spikes: float32 [3, 8192, 512], P(None, ('dom', 'row')), may hold values from -0.1875 to 0.1875
- inverses: float32 [8, 1024, 1024], P('dom', 'row'), may hold values from -1 to 2
Outputs:
- solution: float32 [8192, 128], P(('dom', 'row'))
All inputs are finite; a program needn't handle non-finite values.
Results may differ from a plain program's by a relative error of at most 0.0001.
Values sent between devices are 32-bit elements; how exact they have to be, the bound alone decides.
A program may use at most 64 MiB of HBM per device.

v0:
```python
import jax
import jax.numpy as jnp
from jax import lax
from jax.sharding import PartitionSpec as P

exact_mode = lax.Precision.HIGHEST


def swapped(value, axis, bit):
    return lax.ppermute(value, axis, [(i, i ^ 1 << bit) for i in range(lax.axis_size(axis))])


def shifted(value, axis, steps):
    count = lax.axis_size(axis)
    initial, last = (max(0, -steps), min(count, count - steps))
    return lax.ppermute(value, axis, [(source, source + steps) for source in range(initial, last)])


def pair_spread(solved_rows, offset_in, half_group, level_at):
    holding = offset_in == half_group
    for bit_index in range(level_at, -1, -1):
        partner = swapped(solved_rows, "dom", bit_index)
        solved_rows = jnp.where(holding, solved_rows, partner)
        holding = offset_in % (1 << bit_index) == 0
    return solved_rows


def spread_solution(solved_rows, offset_in, half_group, level_at):
    return pair_spread(solved_rows, offset_in, half_group, level_at)


def body(right_side, spikes, inverses):
    row_count = lax.axis_size("row")
    dom_at = lax.axis_index("dom")
    row_at = lax.axis_index("row")
    local_rows, columns = right_side.shape
    spike_cols = spikes.shape[2]
    tip_devices = spike_cols // local_rows
    inverse_rows = inverses[0]
    is_top = row_at < tip_devices
    is_bottom = row_at >= row_count - tip_devices
    is_holder = is_top | is_bottom
    slot_at = jnp.where(
        is_top, spike_cols + row_at * local_rows, (row_at - (row_count - tip_devices)) * local_rows
    )
    slot_at = jnp.clip(slot_at, 0, 2 * spike_cols - local_rows)
    whole_inverse = lax.all_gather(inverse_rows, "row", axis=0, tiled=True)
    my_columns = lax.dynamic_slice_in_dim(whole_inverse, slot_at, local_rows, 1)
    current = right_side
    for level_at in range(spikes.shape[0]):
        half_group = 1 << level_at
        offset_in = dom_at % (2 * half_group)
        left_block = offset_in < half_group
        incoming = shifted(current, "dom", 1)
        tip_slab = jnp.where(is_top, current, incoming)
        held_slab = jnp.where(is_holder, tip_slab, 0.0)
        solved_rows = lax.psum_scatter(
            jnp.dot(
                my_columns, held_slab, precision=exact_mode, preferred_element_type=jnp.float32
            ),
            "row",
            scatter_dimension=0,
            tiled=True,
        )
        solved_rows = spread_solution(solved_rows, offset_in, half_group, level_at)
        spike_level = spikes[level_at]
        all_rows = lax.all_gather(solved_rows, "row", axis=0, tiled=True)
        needed_half = lax.dynamic_slice_in_dim(
            all_rows, jnp.where(left_block, spike_cols, 0), spike_cols, 0
        )
        update = jnp.dot(
            spike_level, needed_half, precision=exact_mode, preferred_element_type=jnp.float32
        )
        current = current - update
    return current


def solution(mesh):
    in_specs = (P(("dom", "row"), None), P(None, ("dom", "row"), None), P("dom", "row", None))
    out_specs = P(("dom", "row"), None)
    return jax.shard_map(body, mesh=mesh, in_specs=in_specs, out_specs=out_specs, check_vma=False)
```

profile of v0, /device:TPU:3, one launch (start us, length us, event | category | flops | bytes accessed | tf_op | source)
XLA Modules:
  0.0 202.6 jit_solution(13710292264732506317)
XLA Ops:
  6.5 0.7 all-gather.3.cloned.1.call-update
  7.3 1.0 copy.6
  8.3 3.2 %collective-permute-start = (f32[256,128]{0,1:T(8,128)S(1)}, f32[256,128]{0,1:T(8,128)S(1)}, u32[]{:S(2)}, u32[]{:S(2)}) collective-permute-start(f32[256,128]{0,1:T(8,128)S(1)} %copy.6), channel_id=1, source_target_pairs={{0,4},{4,8},{8,12},{12,16},{16,20},{20,24},{24,28},{1,5},{5,9},{9,... | collective-permute-start | bytes 393224 | tf_op jit(solution)/shard_map/ppermute | solution.py:16
  11.5 3.1 %collective-permute-done = f32[256,128]{0,1:T(8,128)S(1)} collective-permute-done((f32[256,128]{0,1:T(8,128)S(1)}, f32[256,128]{0,1:T(8,128)S(1)}, u32[]{:S(2)}, u32[]{:S(2)}) %collective-permute-start) | collective-permute-done | bytes 131104 | tf_op jit(solution)/shard_map/ppermute | solution.py:16
  14.6 30.5 %all-gather.3.cloned.1.call-done = f32[1,1024,1024]{2,1,0:T(8,128)} async-done(((f32[1,256,1024]{2,1,0:T(8,128)}), f32[1,1024,1024]{2,1,0:T(8,128)}) %all-gather.3.cloned.1.call-update) | async-done | bytes 4194320 | tf_op jit(solution)/shard_map/all_gather | solution.py:47
  45.1 3.0 %fusion.7 = f32[1024,128]{1,0:T(8,128)} fusion(f32[1,1024,1024]{2,1,0:T(8,128)} %all-gather.3.cloned.1.call-done, s32[]{:T(128)S(6)} %min.4, f32[256,128]{0,1:T(8,128)S(1)} %copy.6, f32[256,128]{0,1:T(8,128)S(1)} %collective-permute-done, pred[]{:T(512)S(6)} %lt.43, pred[]{:T(512)S(6)} %or.3), kind=kOutput, calls=%fused_computation.10 | convolution fusion | flops 402718720 | bytes 1835014 | tf_op jit(solution)/shard_map/dot_general | solution.py:58
  48.2 21.5 %reduce-scatter.4.cloned.1.call-done = f32[256,128]{1,0:T(8,128)} async-done(((f32[1024,128]{1,0:T(8,128)}), f32[256,128]{1,0:T(8,128)}) %reduce-scatter.4.cloned.1.call-update) | async-done | bytes 131088 | tf_op jit(solution)/shard_map/reduce_scatter | solution.py:57
  70.0 4.3 %collective-permute-done.1 = f32[256,128]{1,0:T(8,128)S(1)} collective-permute-done((f32[256,128]{1,0:T(8,128)}, f32[256,128]{1,0:T(8,128)S(1)}, u32[]{:S(2)}, u32[]{:S(2)}) %collective-permute-start.1) | collective-permute-done | bytes 131104 | tf_op jit(solution)/shard_map/ppermute | solution.py:10
  74.3 0.9 broadcast_select_fusion.5
  75.2 7.9 %all_gather.13 = f32[1024,128]{1,0:T(8,128)S(1)} all-gather(f32[256,128]{1,0:T(8,128)S(1)} %broadcast_select_fusion.5), channel_id=1, replica_groups=mesh['dom'=8,'row'=4] {'row'}, dimensions={0}, use_global_device_ids=true | all-gather | bytes 655360 | tf_op jit(solution)/shard_map/all_gather | solution.py:67
  83.1 0.6 fusion.2
  83.7 2.2 %collective-permute-start.2 = (f32[256,128]{0,1:T(8,128)S(1)}, f32[256,128]{0,1:T(8,128)S(1)}, u32[]{:S(2)}, u32[]{:S(2)}) collective-permute-start(f32[256,128]{0,1:T(8,128)S(1)} %fusion.2), channel_id=1, source_target_pairs={{0,4},{4,8},{8,12},{12,16},{16,20},{20,24},{24,28},{1,5},{5,9},{9,... | collective-permute-start | bytes 393224 | tf_op jit(solution)/shard_map/ppermute | solution.py:16
  85.9 4.6 %collective-permute-done.2 = f32[256,128]{0,1:T(8,128)S(1)} collective-permute-done((f32[256,128]{0,1:T(8,128)S(1)}, f32[256,128]{0,1:T(8,128)S(1)}, u32[]{:S(2)}, u32[]{:S(2)}) %collective-permute-start.2) | collective-permute-done | bytes 131104 | tf_op jit(solution)/shard_map/ppermute | solution.py:16
  90.6 3.0 %fusion.5 = f32[1024,128]{1,0:T(8,128)} fusion(f32[1,1024,1024]{2,1,0:T(8,128)} %all-gather.3.cloned.1.call-done, s32[]{:T(128)S(6)} %min.4, f32[256,128]{0,1:T(8,128)S(1)} %fusion.2, f32[256,128]{0,1:T(8,128)S(1)} %collective-permute-done.2, pred[]{:T(512)S(6)} %lt.43, pred[]{:T(512)S(6)} %or.3), kind=kOutput, calls=%fused_computation.8 | convolution fusion | flops 402718720 | bytes 1835014 | tf_op jit(solution)/shard_map/dot_general | solution.py:58
  93.7 22.8 %reduce-scatter.6.cloned.1.call-done = f32[256,128]{1,0:T(8,128)} async-done(((f32[1024,128]{1,0:T(8,128)}), f32[256,128]{1,0:T(8,128)}) %reduce-scatter.6.cloned.1.call-update) | async-done | bytes 131088 | tf_op jit(solution)/shard_map/reduce_scatter | solution.py:57
  116.5 1.2 collective-permute-start.3
  117.7 3.4 %collective-permute-done.3 = f32[256,128]{1,0:T(8,128)S(1)} collective-permute-done((f32[256,128]{1,0:T(8,128)}, f32[256,128]{1,0:T(8,128)S(1)}, u32[]{:S(2)}, u32[]{:S(2)}) %collective-permute-start.3) | collective-permute-done | bytes 131104 | tf_op jit(solution)/shard_map/ppermute | solution.py:10
  121.5 3.6 %collective-permute-done.4 = f32[256,128]{1,0:T(8,128)S(1)} collective-permute-done((f32[256,128]{1,0:T(8,128)S(1)}, f32[256,128]{1,0:T(8,128)S(1)}, u32[]{:S(2)}, u32[]{:S(2)}) %collective-permute-start.4) | collective-permute-done | bytes 131104 | tf_op jit(solution)/shard_map/ppermute | solution.py:10
  125.0 9.0 %all_gather.14 = f32[1024,128]{1,0:T(8,128)S(1)} all-gather(f32[256,128]{1,0:T(8,128)S(1)} %broadcast_select_fusion.4), channel_id=1, replica_groups=mesh['dom'=8,'row'=4] {'row'}, dimensions={0}, use_global_device_ids=true | all-gather | bytes 655360 | tf_op jit(solution)/shard_map/all_gather | solution.py:67
  134.1 0.6 fusion.1
  134.7 4.0 %collective-permute-start.5 = (f32[256,128]{0,1:T(8,128)S(1)}, f32[256,128]{0,1:T(8,128)S(1)}, u32[]{:S(2)}, u32[]{:S(2)}) collective-permute-start(f32[256,128]{0,1:T(8,128)S(1)} %fusion.1), channel_id=1, source_target_pairs={{0,4},{4,8},{8,12},{12,16},{16,20},{20,24},{24,28},{1,5},{5,9},{9,... | collective-permute-start | bytes 393224 | tf_op jit(solution)/shard_map/ppermute | solution.py:16
  138.7 2.8 %collective-permute-done.5 = f32[256,128]{0,1:T(8,128)S(1)} collective-permute-done((f32[256,128]{0,1:T(8,128)S(1)}, f32[256,128]{0,1:T(8,128)S(1)}, u32[]{:S(2)}, u32[]{:S(2)}) %collective-permute-start.5) | collective-permute-done | bytes 131104 | tf_op jit(solution)/shard_map/ppermute | solution.py:16
  141.5 3.0 %fusion.3 = f32[1024,128]{1,0:T(8,128)} fusion(f32[1,1024,1024]{2,1,0:T(8,128)} %all-gather.3.cloned.1.call-done, s32[]{:T(128)S(6)} %min.4, f32[256,128]{0,1:T(8,128)S(1)} %fusion.1, f32[256,128]{0,1:T(8,128)S(1)} %collective-permute-done.5, pred[]{:T(512)S(6)} %lt.43, pred[]{:T(512)S(6)} %or.3), kind=kOutput, calls=%fused_computation.6 | convolution fusion | flops 402718720 | bytes 1835014 | tf_op jit(solution)/shard_map/dot_general | solution.py:58
  144.6 23.8 %reduce-scatter.8.cloned.1.call-done = f32[256,128]{1,0:T(8,128)} async-done(((f32[1024,128]{1,0:T(8,128)}), f32[256,128]{1,0:T(8,128)}) %reduce-scatter.8.cloned.1.call-update) | async-done | bytes 131088 | tf_op jit(solution)/shard_map/reduce_scatter | solution.py:57
  168.4 2.1 %collective-permute-start.6 = (f32[256,128]{1,0:T(8,128)}, f32[256,128]{1,0:T(8,128)S(1)}, u32[]{:S(2)}, u32[]{:S(2)}) collective-permute-start(f32[256,128]{1,0:T(8,128)} %reduce-scatter.8.cloned.1.call-done), channel_id=1, source_target_pairs={{0,16},{4,20},{8,24},{12,28},{16,0},{20,4},{24,8},{28,12},{1,17},{... | collective-permute-start | bytes 393224 | tf_op jit(solution)/shard_map/ppermute | solution.py:10
  170.5 6.3 %collective-permute-done.6 = f32[256,128]{1,0:T(8,128)S(1)} collective-permute-done((f32[256,128]{1,0:T(8,128)}, f32[256,128]{1,0:T(8,128)S(1)}, u32[]{:S(2)}, u32[]{:S(2)}) %collective-permute-start.6) | collective-permute-done | bytes 131104 | tf_op jit(solution)/shard_map/ppermute | solution.py:10
  176.8 1.3 collective-permute-start.7
  178.2 2.6 %collective-permute-done.7 = f32[256,128]{1,0:T(8,128)S(1)} collective-permute-done((f32[256,128]{1,0:T(8,128)S(1)}, f32[256,128]{1,0:T(8,128)S(1)}, u32[]{:S(2)}, u32[]{:S(2)}) %collective-permute-start.7) | collective-permute-done | bytes 131104 | tf_op jit(solution)/shard_map/ppermute | solution.py:10
  181.1 3.6 %collective-permute-done.8 = f32[256,128]{1,0:T(8,128)S(1)} collective-permute-done((f32[256,128]{1,0:T(8,128)S(1)}, f32[256,128]{1,0:T(8,128)S(1)}, u32[]{:S(2)}, u32[]{:S(2)}) %collective-permute-start.8) | collective-permute-done | bytes 131104 | tf_op jit(solution)/shard_map/ppermute | solution.py:10
  184.7 10.1 %all_gather.15 = f32[1024,128]{1,0:T(8,128)S(1)} all-gather(f32[256,128]{1,0:T(8,128)S(1)} %broadcast_select_fusion.2), channel_id=1, replica_groups=mesh['dom'=8,'row'=4] {'row'}, dimensions={0}, use_global_device_ids=true | all-gather | bytes 655360 | tf_op jit(solution)/shard_map/all_gather | solution.py:67
  194.7 0.6 fusion
  195.4 0.8 copy.7
  (17 shorter events, 1.2 us)
Async XLA Ops:
  6.5 76.6 %copy-start = (f32[3,256,512]{2,1,0:T(8,128)S(1)}, f32[3,256,512]{2,1,0:T(8,128)}, u32[]{:S(2)}) copy-start(f32[3,256,512]{2,1,0:T(8,128)} %param.4) | copy-start | bytes 4718596
  6.5 38.5 %all-gather.3.cloned.1.call-start = ((), (), s32[]{:S(2)}) async-start(), calls=%async_computation.6 | async-start | bytes 5242880 | tf_op jit(solution)/shard_map/all_gather | solution.py:47
  7.3 62.5 %reduce-scatter.4.cloned.1.call-start = ((), (), s32[]{:S(2)}) async-start(), calls=%async_computation.3 | async-start | bytes 655360 | tf_op jit(solution)/shard_map/reduce_scatter | solution.py:57
  8.3 6.3 %collective-permute-start = (f32[256,128]{0,1:T(8,128)S(1)}, f32[256,128]{0,1:T(8,128)S(1)}, u32[]{:S(2)}, u32[]{:S(2)}) collective-permute-start(f32[256,128]{0,1:T(8,128)S(1)} %copy.6), channel_id=1, source_target_pairs={{0,4},{4,8},{8,12},{12,16},{16,20},{20,24},{24,28},{1,5},{5,9},{9,... | collective-permute-start | bytes 393224 | tf_op jit(solution)/shard_map/ppermute | solution.py:16
  48.1 68.4 %reduce-scatter.6.cloned.1.call-start = ((), (), s32[]{:S(2)}) async-start(), calls=%async_computation.4 | async-start | bytes 655360 | tf_op jit(solution)/shard_map/reduce_scatter | solution.py:57
  69.7 4.6 %collective-permute-start.1 = (f32[256,128]{1,0:T(8,128)}, f32[256,128]{1,0:T(8,128)S(1)}, u32[]{:S(2)}, u32[]{:S(2)}) collective-permute-start(f32[256,128]{1,0:T(8,128)} %reduce-scatter.4.cloned.1.call-done), channel_id=1, source_target_pairs={{0,4},{4,0},{8,12},{12,8},{16,20},{20,16},{24,28},{28,24},{1,5},{5... | collective-permute-start | bytes 393224 | tf_op jit(solution)/shard_map/ppermute | solution.py:10
  83.7 6.8 %collective-permute-start.2 = (f32[256,128]{0,1:T(8,128)S(1)}, f32[256,128]{0,1:T(8,128)S(1)}, u32[]{:S(2)}, u32[]{:S(2)}) collective-permute-start(f32[256,128]{0,1:T(8,128)S(1)} %fusion.2), channel_id=1, source_target_pairs={{0,4},{4,8},{8,12},{12,16},{16,20},{20,24},{24,28},{1,5},{5,9},{9,... | collective-permute-start | bytes 393224 | tf_op jit(solution)/shard_map/ppermute | solution.py:16
  93.6 74.8 %reduce-scatter.8.cloned.1.call-start = ((), (), s32[]{:S(2)}) async-start(), calls=%async_computation.5 | async-start | bytes 655360 | tf_op jit(solution)/shard_map/reduce_scatter | solution.py:57
  116.5 4.6 %collective-permute-start.3 = (f32[256,128]{1,0:T(8,128)}, f32[256,128]{1,0:T(8,128)S(1)}, u32[]{:S(2)}, u32[]{:S(2)}) collective-permute-start(f32[256,128]{1,0:T(8,128)} %reduce-scatter.6.cloned.1.call-done), channel_id=1, source_target_pairs={{0,8},{4,12},{8,0},{12,4},{16,24},{20,28},{24,16},{28,20},{1,9},{5... | collective-permute-start | bytes 393224 | tf_op jit(solution)/shard_map/ppermute | solution.py:10
  121.1 3.9 %collective-permute-start.4 = (f32[256,128]{1,0:T(8,128)S(1)}, f32[256,128]{1,0:T(8,128)S(1)}, u32[]{:S(2)}, u32[]{:S(2)}) collective-permute-start(f32[256,128]{1,0:T(8,128)S(1)} %broadcast_select_fusion.3), channel_id=1, source_target_pairs={{0,4},{4,0},{8,12},{12,8},{16,20},{20,16},{24,28},{28,24},{1,5},{5... | collective-permute-start | bytes 393224 | tf_op jit(solution)/shard_map/ppermute | solution.py:10
  134.7 6.8 %collective-permute-start.5 = (f32[256,128]{0,1:T(8,128)S(1)}, f32[256,128]{0,1:T(8,128)S(1)}, u32[]{:S(2)}, u32[]{:S(2)}) collective-permute-start(f32[256,128]{0,1:T(8,128)S(1)} %fusion.1), channel_id=1, source_target_pairs={{0,4},{4,8},{8,12},{12,16},{16,20},{20,24},{24,28},{1,5},{5,9},{9,... | collective-permute-start | bytes 393224 | tf_op jit(solution)/shard_map/ppermute | solution.py:16
  168.4 8.4 %collective-permute-start.6 = (f32[256,128]{1,0:T(8,128)}, f32[256,128]{1,0:T(8,128)S(1)}, u32[]{:S(2)}, u32[]{:S(2)}) collective-permute-start(f32[256,128]{1,0:T(8,128)} %reduce-scatter.8.cloned.1.call-done), channel_id=1, source_target_pairs={{0,16},{4,20},{8,24},{12,28},{16,0},{20,4},{24,8},{28,12},{1,17},{... | collective-permute-start | bytes 393224 | tf_op jit(solution)/shard_map/ppermute | solution.py:10
  176.8 3.9 %collective-permute-start.7 = (f32[256,128]{1,0:T(8,128)S(1)}, f32[256,128]{1,0:T(8,128)S(1)}, u32[]{:S(2)}, u32[]{:S(2)}) collective-permute-start(f32[256,128]{1,0:T(8,128)S(1)} %broadcast_select_fusion), channel_id=1, source_target_pairs={{0,8},{4,12},{8,0},{12,4},{16,24},{20,28},{24,16},{28,20},{1,9},{5... | collective-permute-start | bytes 393224 | tf_op jit(solution)/shard_map/ppermute | solution.py:10
  180.8 3.9 %collective-permute-start.8 = (f32[256,128]{1,0:T(8,128)S(1)}, f32[256,128]{1,0:T(8,128)S(1)}, u32[]{:S(2)}, u32[]{:S(2)}) collective-permute-start(f32[256,128]{1,0:T(8,128)S(1)} %broadcast_select_fusion.1), channel_id=1, source_target_pairs={{0,4},{4,0},{8,12},{12,8},{16,20},{20,16},{24,28},{28,24},{1,5},{5... | collective-permute-start | bytes 393224 | tf_op jit(solution)/shard_map/ppermute | solution.py:10
Sparse Core Ops, SparseCore 0:
  8.9 36.1 all-gather.2
  48.3 21.4 reduce-scatter.3
  93.8 22.7 reduce-scatter.5
  144.7 23.6 reduce-scatter.7
where the time goes:
time: 204 us; the launch traced here: 203 us
  waiting for transfers between devices  134 us (66%)
  blocking collectives  27 us (13%)
  starting transfers between devices  15 us (7%)
  between operations  13.2 us (6%)
  matrix products  11 us (5%)
    reduce_scatter x3, waiting for transfers between devices, body(): lax.psum_scatter(jnp.dot(my_columns, held_slab, precision=exact_mode, pre...  68.2 us
    all_gather x1, waiting for transfers between devices, body(): whole_inverse = lax.all_gather(inverse_rows, 'row', axis=0, tiled=True)  30.5 us
    all_gather x3, blocking collectives, body(): all_rows = lax.all_gather(solved_rows, 'row', axis=0, tiled=True)  27 us
    ppermute x6, waiting for transfers between devices, swapped(): lax.ppermute(value, axis, [(i, i ^ 1 << bit) for i in range(lax.axis_size...  23.7 us
    ppermute x3, waiting for transfers between devices, shifted(): lax.ppermute(value, axis, [(source, source + steps) for source in range(i...  10.5 us
    ppermute x3, starting transfers between devices, shifted(): lax.ppermute(value, axis, [(source, source + steps) for source in range(i...  9.38 us
    dot_general x3, matrix products, body(): jnp.dot(my_columns, held_slab, precision=exact_mode, preferred_element_ty...  9.12 us
    ppermute x6, starting transfers between devices, swapped(): lax.ppermute(value, axis, [(i, i ^ 1 << bit) for i in range(lax.axis_size...  5.54 us
  transfers between devices with their start and end apart: 13, of which 13 were waited for; matrix products, arithmetic and copies ran while one was open for 0% of the time, Pallas kernels for 0%

commit v1 on v0

v1 whole, which is shorter than its diff:
```python
import functools

import jax
import jax.numpy as jnp
from jax import lax
from jax.experimental import pallas as pl
from jax.experimental.pallas import tpu as pltpu
from jax.sharding import PartitionSpec as P

PARTS = 4


def split_pair(value):
    high = value.astype(jnp.bfloat16)
    low = (value - high.astype(jnp.float32)).astype(jnp.bfloat16)
    return high, low


def bf_dot(left, right):
    return jnp.dot(left, right, preferred_element_type=jnp.float32)


def kernel(
    row_count,
    right_ref,
    spikes_ref,
    inverse_ref,
    out_ref,
    right_buf,
    spike_buf,
    inverse_buf,
    inv_hi,
    inv_lo,
    spk_hi,
    spk_lo,
    cur,
    tips,
    piece,
    halves,
    last,
    local_sem,
    pair_send,
    pair_recv,
    a_send,
    a_recv,
    b_send,
    b_recv,
):
    levels, rows, depth = spikes_ref.shape
    columns = right_ref.shape[1]
    half_columns = columns // 2
    inv_rows = inverse_ref.shape[1]
    nodes = row_count // 2
    half_nodes = nodes // 2
    dom = lax.axis_index("dom")
    row = lax.axis_index("row")
    core = lax.rem(row, 2)
    node = row // 2
    other = 1 - core
    lane = lax.broadcasted_iota(jnp.int32, (1, columns), 1)

    def place(dom_at, node_at):
        return {"dom": dom_at, "row": 2 * node_at + core}

    sibling = {"dom": dom, "row": 2 * node + other}

    loads = [
        (right_ref, right_buf.at[core]),
        (inverse_ref.at[0], inverse_buf.at[core]),
    ] + [(spikes_ref.at[l], spike_buf.at[l, core]) for l in range(levels)]
    own, pair = [], []
    for index, (source, target) in enumerate(loads):
        send = pltpu.make_async_remote_copy(
            src_ref=source,
            dst_ref=target,
            send_sem=pair_send.at[index],
            recv_sem=pair_recv.at[index],
            device_id=sibling,
        )
        send.start()
        pair.append(send)
        copy = pltpu.make_async_copy(source, target, local_sem.at[index])
        copy.start()
        own.append(copy)

    def loaded(index):
        own[index].wait()
        pair[index].wait_recv()

    own_lanes = (lane < half_columns) == (core == 0)
    loaded(0)
    cur[0] = jnp.where(
        own_lanes, right_buf[core], pltpu.roll(right_buf[other], half_columns, 1)
    )

    def copy_to(source, target, send_sem, recv_sem, where):
        return pltpu.make_async_remote_copy(
            src_ref=source,
            dst_ref=target,
            send_sem=send_sem,
            recv_sem=recv_sem,
            device_id=where,
        )

    tip_chunk = rows // PARTS
    piece_chunk = inv_rows // PARTS
    tip_cut = [pl.ds(c * tip_chunk, tip_chunk) for c in range(PARTS)]
    piece_cut = [pl.ds(c * piece_chunk, piece_chunk) for c in range(PARTS)]
    waits = []

    def send_tips(source, slot, sem_at, c, where):
        copy_to(
            source.at[tip_cut[c]],
            tips.at[slot, tip_cut[c]],
            a_send.at[sem_at],
            a_recv.at[slot, c],
            where,
        ).start()

    def wait_tips(slot, c):
        copy_to(
            tips.at[slot, tip_cut[c]],
            tips.at[slot, tip_cut[c]],
            a_send.at[0],
            a_recv.at[slot, c],
            sibling,
        ).wait_recv()

    def packed(left, right):
        half = left.shape[0] // 2
        low = lane < half_columns
        straight = jnp.where(low, left[:half], right[half:])
        crossed = jnp.where(low, left[half:], right[:half])
        return straight + pltpu.roll(crossed, half_columns, 1)

    def product(hi_ref, lo_ref, messages):
        left = right = None
        for at, message in messages:
            high, low = split_pair(message)
            both = jnp.concatenate([high, low], axis=1)
            sums = []
            for side in range(2):
                cut = slice(at + side * rows, at + (side + 1) * rows)
                wide = bf_dot(hi_ref[:, cut], both)
                thin = bf_dot(lo_ref[:, cut], high)
                sums.append(wide[:, :columns] + (wide[:, columns:] + thin))
            left = sums[0] if left is None else left + sums[0]
            right = sums[1] if right is None else right + sums[1]
        return packed(left, right)

    def run_level(level):
        group = 1 << level
        offset = lax.rem(dom, 2 * group)
        base = dom - offset
        is_left = offset < group
        is_solver = offset == group
        solver_dom = base + group
        entry = max(group - 2, 0)
        from_bottom = (offset == group - 1) & (node == nodes - 1)

        @pl.when(from_bottom)
        def _():
            for c in range(PARTS):
                send_tips(cur.at[level], 0, 2 * nodes * level, c, place(dom + 1, nodes - 1))

        def across(step):
            return lax.rem(node + step, nodes)

        @pl.when(is_solver & (node == 0))
        def _():
            for c in range(PARTS):
                for step in range(1, nodes):
                    send_tips(cur.at[level], 1, 2 * nodes * level + step, c, place(dom, step))

        if level == 0:
            loaded(1)
            for side in range(2):
                high, low = split_pair(inverse_buf[side])
                at = slice(side * inv_rows, (side + 1) * inv_rows)
                inv_hi[at], inv_lo[at] = high, low

        relative = jnp.where(
            is_left, (offset // 2) * 2 + lax.rem(offset, 2) - entry, offset - group
        )
        if group >= 2:
            high_part = offset // 2
            flipped = (group // 2 - 1 - high_part) * 2 + lax.rem(offset, 2)
            relative = jnp.where(is_left, flipped, offset - group)
        else:
            relative = offset - offset
        piece_at = lax.rem(node, half_nodes)
        holder = jnp.where(is_left, node >= half_nodes, node < half_nodes)

        def spread(source, c, wait):
            def go(copy):
                copy.wait_send() if wait else copy.start()

            cut = piece_cut[c]
            target = halves.at[level, pl.ds(piece_at * inv_rows + c * piece_chunk, piece_chunk)]
            if wait:
                source, target = source, halves.at[level, pl.ds(piece_at * inv_rows, inv_rows)]
            else:
                source = source.at[cut]
            recv = b_recv.at[level, piece_at, c]
            bit, number = group // 2, 0
            while bit >= 1:
                child = relative + bit
                if group >= 2:
                    left_child = (group // 2 - 1 - child // 2) * 2 + lax.rem(child, 2)
                else:
                    left_child = child
                child_dom = base + jnp.where(is_left, left_child, group + child)

                @pl.when(lax.rem(relative, 2 * bit) == 0)
                def _(number=number, child_dom=child_dom):
                    go(copy_to(source, target, b_send.at[level, number], recv, place(child_dom, node)))

                bit //= 2
                number += 1
            for step in range(1, nodes):
                go(
                    copy_to(
                        source,
                        target,
                        b_send.at[level, levels + step],
                        recv,
                        place(dom, across(step)),
                    )
                )

        def to_left(c, wait):
            whole = pl.ds(piece_at * inv_rows, inv_rows)
            part = pl.ds(piece_at * inv_rows + c * piece_chunk, piece_chunk)
            copy = copy_to(
                piece if wait else piece.at[piece_cut[c]],
                halves.at[level, whole if wait else part],
                b_send.at[level, levels],
                b_recv.at[level, piece_at, c],
                place(base + entry, node),
            )
            copy.wait_send() if wait else copy.start()

        @pl.when(is_solver)
        def _():
            for c in range(PARTS):
                wait_tips(0, c)

                @pl.when(node == nodes - 1)
                def _():
                    for step in range(nodes - 1):
                        send_tips(
                            tips.at[0], 0, 2 * nodes * level + nodes + step, c, place(dom, step)
                        )

            @pl.when(node == 0)
            def _():
                tips[1] = cur[level]

            @pl.when(node != 0)
            def _():
                for c in range(PARTS):
                    wait_tips(1, c)

            piece[...] = product(inv_hi, inv_lo, [(0, tips[0]), (depth, tips[1])])

            @pl.when(node < half_nodes)
            def _():
                for c in range(PARTS):
                    spread(piece, c, False)
                halves[level, pl.ds(piece_at * inv_rows, inv_rows)] = piece[...]

            @pl.when(node >= half_nodes)
            def _():
                for c in range(PARTS):
                    to_left(c, False)

        loaded(2 + level)
        for side in range(2):
            high, low = split_pair(spike_buf[level, side])
            at = slice(side * rows, (side + 1) * rows)
            for value, target in ((high, spk_hi), (low, spk_lo)):
                if half_nodes > 1:
                    blocks = [
                        value[:, (2 * i + part) * inv_rows : (2 * i + part + 1) * inv_rows]
                        for part in range(2)
                        for i in range(half_nodes)
                    ]
                    value = jnp.concatenate(blocks, axis=1)
                target[level, at] = value

        for c in range(PARTS):
            for index in range(half_nodes):
                mine = is_solver & (node == index)
                forward = holder & (piece_at == index) & ~mine

                @pl.when(~mine)
                def _():
                    part = halves.at[level, pl.ds(index * inv_rows + c * piece_chunk, piece_chunk)]
                    copy_to(
                        part, part, b_send.at[0, 0], b_recv.at[level, index, c], sibling
                    ).wait_recv()

                @pl.when(forward)
                def _():
                    spread(halves.at[level, pl.ds(index * inv_rows, inv_rows)], c, False)

        update = product(spk_hi.at[level], spk_lo.at[level], [(0, halves[level])])
        cur[level + 1] = cur[level] - update

        def finish():
            @pl.when(from_bottom)
            def _():
                copy_to(
                    cur.at[level], tips.at[0], a_send.at[2 * nodes * level], a_recv.at[0, 0],
                    place(dom + 1, nodes - 1),
                ).wait_send()

            @pl.when(is_solver & (node == 0))
            def _():
                for step in range(1, nodes):
                    copy_to(
                        cur.at[level], tips.at[1], a_send.at[2 * nodes * level + step],
                        a_recv.at[1, 0], place(dom, step),
                    ).wait_send()

            @pl.when(is_solver & (node == nodes - 1))
            def _():
                for step in range(nodes - 1):
                    copy_to(
                        tips.at[0], tips.at[0], a_send.at[2 * nodes * level + nodes + step],
                        a_recv.at[0, 0], place(dom, step),
                    ).wait_send()

            @pl.when(is_solver & (node >= half_nodes))
            def _():
                to_left(0, True)

            @pl.when(holder)
            def _():
                spread(halves.at[level, pl.ds(piece_at * inv_rows, inv_rows)], 0, True)

        waits.append(finish)

    for level in range(levels):
        run_level(level)

    swap = copy_to(cur.at[levels], last, pair_send.at[levels + 2], pair_recv.at[levels + 2], sibling)
    swap.start()
    for finish in waits:
        finish()
    for send in pair:
        send.wait_send()
    swap.wait()
    out_ref[...] = jnp.where(own_lanes, cur[levels], pltpu.roll(last[...], half_columns, 1))


def body(right_side, spikes, inverses):
    row_count = lax.axis_size("row")
    rows, columns = right_side.shape
    levels, _, depth = spikes.shape
    inv_rows = inverses.shape[1]
    nodes = row_count // 2
    f32, bf16 = jnp.float32, jnp.bfloat16
    dma = pltpu.SemaphoreType.DMA
    return pl.pallas_call(
        functools.partial(kernel, row_count),
        out_shape=jax.ShapeDtypeStruct((rows, columns), f32),
        in_specs=[pl.BlockSpec(memory_space=pl.ANY)] * 3,
        out_specs=pl.BlockSpec(memory_space=pltpu.VMEM),
        scratch_shapes=[
            pltpu.VMEM((2, rows, columns), f32),
            pltpu.VMEM((levels, 2, rows, depth), f32),
            pltpu.VMEM((2, inv_rows, 2 * depth), f32),
            pltpu.VMEM((2 * inv_rows, 2 * depth), bf16),
            pltpu.VMEM((2 * inv_rows, 2 * depth), bf16),
            pltpu.VMEM((levels, 2 * rows, depth), bf16),
            pltpu.VMEM((levels, 2 * rows, depth), bf16),
            pltpu.VMEM((levels + 1, rows, columns), f32),
            pltpu.VMEM((2, rows, columns), f32),
            pltpu.VMEM((inv_rows, columns), f32),
            pltpu.VMEM((levels, depth // 2, columns), f32),
            pltpu.VMEM((rows, columns), f32),
            dma((levels + 2,)),
            dma((levels + 3,)),
            dma((levels + 3,)),
            dma((2 * nodes * levels,)),
            dma((2, PARTS)),
            dma((levels, levels + nodes)),
            dma((levels, nodes // 2, PARTS)),
        ],
        compiler_params=pltpu.CompilerParams(
            has_side_effects=True, vmem_limit_bytes=48 * 1024 * 1024
        ),
        cost_estimate=pl.CostEstimate(
            flops=2 * 6 * (2 * rows * depth * columns * levels),
            bytes_accessed=4 * (spikes.size + inverses.size + 2 * right_side.size),
            transcendentals=0,
        ),
    )(right_side, spikes, inverses)


def solution(mesh):
    in_specs = (P(("dom", "row"), None), P(None, ("dom", "row"), None), P("dom", "row", None))
    out_specs = P(("dom", "row"), None)
    return jax.shard_map(body, mesh=mesh, in_specs=in_specs, out_specs=out_specs, check_vma=False)
```

time: 204 us -> 60.3 us (0.30)
  waiting for transfers between devices: 134 us -> 0 us
  Pallas kernels: 0 us -> 55.9 us
  blocking collectives: 27 us -> 0 us
  starting transfers between devices: 15 us -> 0 us
  between operations: 13.2 us -> 0.01 us
  matrix products: 11 us -> 0 us
  local copies, waits for them, and re-layouts: 1.76 us -> 4.19 us
    reduce_scatter x3 -> x0, waiting for transfers between devices: 68.2 us -> none  [body(): lax.psum_scatter(jnp.dot(my_columns, held_slab, precision=exact_mode, pre...]
    pallas_call x0 -> x1, Pallas kernels: none -> 55.9 us  [body(): pl.pallas_call(functools.partial(kernel, row_count), out_shape=jax.ShapeD...]
    ppermute x9 -> x0, waiting for transfers between devices: 34.2 us -> none  [the longest x6 23.7 us: swapped(): lax.ppermute(value, axis, [(i, i ^ 1 << bit) for i in range(lax.axis_size...]
    all_gather x1 -> x0, waiting for transfers between devices: 30.5 us -> none  [body(): whole_inverse = lax.all_gather(inverse_rows, 'row', axis=0, tiled=True)]
    all_gather x3 -> x0, blocking collectives: 27 us -> none  [body(): all_rows = lax.all_gather(solved_rows, 'row', axis=0, tiled=True)]
    ppermute x9 -> x0, starting transfers between devices: 14.9 us -> none  [the longest x3 9.38 us: shifted(): lax.ppermute(value, axis, [(source, source + steps) for source in range(i...]
    dot_general x6 -> x0, matrix products: 11 us -> none  [the longest x3 9.12 us: body(): jnp.dot(my_columns, held_slab, precision=exact_mode, preferred_element_ty...]
    unnamed x3 -> x7, local copies, waits for them, and re-layouts: 1 us -> 4.19 us
  transfers between devices with their start and end apart: 13 -> 0, of which waited for: 13 -> 0; matrix products, arithmetic and copies ran while one was open for 0% -> 0% of each run, Pallas kernels for 0% -> 0%
where the time goes in v1:
time: 60.3 us; the launch traced here: 60.1 us
  Pallas kernels  55.9 us (93%)
  local copies, waits for them, and re-layouts  4.19 us (7%)
    pallas_call x1, Pallas kernels, body(): pl.pallas_call(functools.partial(kernel, row_count), out_shape=jax.ShapeD...  55.9 us
    unnamed x7, local copies, waits for them, and re-layouts  4.19 us

profile of v1, /device:TPU:3, one launch (start us, length us, event | category | flops | bytes accessed | tf_op | source)
XLA Modules:
  0.0 60.1 jit_solution(15421172343501364188)
XLA Ops:
  0.0 0.0 copy-start
  0.0 1.4 %copy-done = f32[3,256,512]{2,1,0:T(8,128)S(1)} copy-done((f32[3,256,512]{2,1,0:T(8,128)S(1)}, f32[3,256,512]{2,1,0:T(8,128)}, u32[]{:S(2)}) %copy-start) | copy-done | bytes 1572888
  1.4 0.0 copy-start.1
  1.4 1.2 %copy-done.1 = f32[1,256,1024]{2,1,0:T(8,128)S(1)} copy-done((f32[1,256,1024]{2,1,0:T(8,128)S(1)}, f32[1,256,1024]{2,1,0:T(8,128)}, u32[]{:S(2)}) %copy-start.1) | copy-done | bytes 1048600
  2.6 0.0 copy-start.2
  2.6 0.9 %copy-done.2 = f32[256,128]{1,0:T(8,128)S(1)} copy-done((f32[256,128]{1,0:T(8,128)S(1)}, f32[256,128]{1,0:T(8,128)}, u32[]{:S(2)}) %copy-start.2) | copy-done | bytes 131096
  3.5 55.9 %shard_map.37 = f32[256,128]{1,0:T(8,128)S(1)} custom-call(f32[256,128]{1,0:T(8,128)S(1)} %copy-done.2, f32[3,256,512]{2,1,0:T(8,128)S(1)} %copy-done, f32[1,256,1024]{2,1,0:T(8,128)S(1)} %copy-done.1), custom_call_target="tpu_custom_call" | custom-call | flops 1207959552 | bytes 2883584 | tf_op jit(solution)/shard_map/pallas_call | solution.py:365
  59.5 0.7 %copy.5 = f32[256,128]{1,0:T(8,128)} copy(f32[256,128]{1,0:T(8,128)S(1)} %shard_map.37) | data formatting | bytes 262144
Async XLA Ops:
  0.0 1.4 %copy-start = (f32[3,256,512]{2,1,0:T(8,128)S(1)}, f32[3,256,512]{2,1,0:T(8,128)}, u32[]{:S(2)}) copy-start(f32[3,256,512]{2,1,0:T(8,128)} %spikes_ref.1) | copy-start | bytes 4718596
  1.4 1.2 %copy-start.1 = (f32[1,256,1024]{2,1,0:T(8,128)S(1)}, f32[1,256,1024]{2,1,0:T(8,128)}, u32[]{:S(2)}) copy-start(f32[1,256,1024]{2,1,0:T(8,128)} %inverse_ref.1) | copy-start | bytes 3145732
  2.6 0.9 %copy-start.2 = (f32[256,128]{1,0:T(8,128)S(1)}, f32[256,128]{1,0:T(8,128)}, u32[]{:S(2)}) copy-start(f32[256,128]{1,0:T(8,128)} %right_ref.1) | copy-start | bytes 393220

commit v2 on v1

--- a/solution.py
+++ b/solution.py
@@ -7,7 +7,8 @@
 from jax.experimental.pallas import tpu as pltpu
 from jax.sharding import PartitionSpec as P
 
-PARTS = 4
+PARTS = 8
+VMEM_LIMIT = 63 * 1024 * 1024 + 896 * 1024
 
 
 def split_pair(value):
@@ -64,6 +65,62 @@
 
     sibling = {"dom": dom, "row": 2 * node + other}
 
+    def position(level):
+        group = 1 << level
+        offset = lax.rem(dom, 2 * group)
+        is_left = offset < group
+        if group >= 2:
+            flipped = (group // 2 - 1 - offset // 2) * 2 + lax.rem(offset, 2)
+            relative = jnp.where(is_left, flipped, offset - group)
+        else:
+            relative = offset - offset
+        holder = jnp.where(is_left, node >= half_nodes, node < half_nodes)
+        return group, offset, dom - offset, is_left, relative, holder
+
+    def tree_dom(group, base, is_left, relative):
+        if group >= 2:
+            left = (group // 2 - 1 - relative // 2) * 2 + lax.rem(relative, 2)
+        else:
+            left = relative
+        return base + jnp.where(is_left, left, group + relative)
+
+    barrier = pltpu.get_barrier_semaphore()
+
+    def greet(where):
+        pl.semaphore_signal(barrier, inc=1, device_id=where)
+
+    expected = nodes + 0 * dom
+    greet(sibling)
+    for step in range(1, nodes):
+        greet(place(dom, lax.rem(node + step, nodes)))
+    dom_count = lax.axis_size("dom")
+
+    @pl.when((node == nodes - 1) & (dom > 0))
+    def _():
+        greet(place(dom - 1, nodes - 1))
+
+    def count(condition):
+        return jnp.where(condition, 1, 0)
+
+    expected += count((node == nodes - 1) & (dom < dom_count - 1))
+    for level in range(levels):
+        group, offset, base, is_left, relative, holder = position(level)
+
+        @pl.when((offset == max(group - 2, 0)) & (node >= half_nodes))
+        def _():
+            greet(place(base + group, node))
+
+        expected += count((offset == group) & (node >= half_nodes))
+        bit = group // 2
+        while bit >= 1:
+            @pl.when(holder & (lax.rem(relative, 2 * bit) == bit))
+            def _(bit=bit):
+                greet(place(tree_dom(group, base, is_left, relative - bit), node))
+
+            expected += count(holder & (lax.rem(relative, 2 * bit) == 0))
+            bit //= 2
+    pl.semaphore_wait(barrier, expected)
+
     loads = [
         (right_ref, right_buf.at[core]),
         (inverse_ref.at[0], inverse_buf.at[core]),
@@ -149,12 +206,8 @@
         return packed(left, right)
 
     def run_level(level):
-        group = 1 << level
-        offset = lax.rem(dom, 2 * group)
-        base = dom - offset
-        is_left = offset < group
+        group, offset, base, is_left, relative, holder = position(level)
         is_solver = offset == group
-        solver_dom = base + group
         entry = max(group - 2, 0)
         from_bottom = (offset == group - 1) & (node == nodes - 1)
 
@@ -179,17 +232,7 @@
                 at = slice(side * inv_rows, (side + 1) * inv_rows)
                 inv_hi[at], inv_lo[at] = high, low
 
-        relative = jnp.where(
-            is_left, (offset // 2) * 2 + lax.rem(offset, 2) - entry, offset - group
-        )
-        if group >= 2:
-            high_part = offset // 2
-            flipped = (group // 2 - 1 - high_part) * 2 + lax.rem(offset, 2)
-            relative = jnp.where(is_left, flipped, offset - group)
-        else:
-            relative = offset - offset
         piece_at = lax.rem(node, half_nodes)
-        holder = jnp.where(is_left, node >= half_nodes, node < half_nodes)
 
         def spread(source, c, wait):
             def go(copy):
@@ -205,11 +248,7 @@
             bit, number = group // 2, 0
             while bit >= 1:
                 child = relative + bit
-                if group >= 2:
-                    left_child = (group // 2 - 1 - child // 2) * 2 + lax.rem(child, 2)
-                else:
-                    left_child = child
-                child_dom = base + jnp.where(is_left, left_child, group + child)
+                child_dom = tree_dom(group, base, is_left, child)
 
                 @pl.when(lax.rem(relative, 2 * bit) == 0)
                 def _(number=number, child_dom=child_dom):
@@ -389,7 +428,7 @@
             dma((levels, nodes // 2, PARTS)),
         ],
         compiler_params=pltpu.CompilerParams(
-            has_side_effects=True, vmem_limit_bytes=48 * 1024 * 1024
+            has_side_effects=True, vmem_limit_bytes=VMEM_LIMIT, collective_id=0
         ),
         cost_estimate=pl.CostEstimate(
             flops=2 * 6 * (2 * rows * depth * columns * levels),

time: 60.3 us -> 53.5 us (0.89)
  Pallas kernels: 55.9 us -> 51.8 us
  local copies, waits for them, and re-layouts: 4.19 us -> 1.57 us
    pallas_call x1, Pallas kernels: 55.9 us -> 51.8 us  [body(): pl.pallas_call(functools.partial(kernel, row_count), out_shape=jax.ShapeD...]
    unnamed x7 -> x1, local copies, waits for them, and re-layouts: 4.19 us -> 1.57 us
where the time goes in v2:
time: 53.5 us; the launch traced here: 53.3 us
  Pallas kernels  51.8 us (97%)
  local copies, waits for them, and re-layouts  1.57 us (3%)
    pallas_call x1, Pallas kernels, body(): pl.pallas_call(functools.partial(kernel, row_count), out_shape=jax.ShapeD...  51.8 us
    unnamed x1, local copies, waits for them, and re-layouts  1.57 us

profile of v2, /device:TPU:3, one launch (start us, length us, event | category | flops | bytes accessed | tf_op | source)
XLA Modules:
  0.0 53.3 jit_solution(6837560993742026446)
XLA Ops:
  0.0 51.8 %shard_map.37 = f32[256,128]{1,0:T(8,128)} custom-call(f32[256,128]{1,0:T(8,128)} %right_ref.1, f32[3,256,512]{2,1,0:T(8,128)} %spikes_ref.1, f32[1,256,1024]{2,1,0:T(8,128)} %inverse_ref.1), custom_call_target="tpu_custom_call" | custom-call | flops 1207959552 | bytes 2883584 | tf_op jit(solution)/shard_map/pallas_call | solution.py:404
  51.8 1.6 %copy.5 = f32[256,128]{1,0:T(8,128)} copy(f32[256,128]{1,0:T(8,128)} %shard_map.37) | data formatting | bytes 262144

commit v3 on v2

--- a/solution.py
+++ b/solution.py
@@ -46,6 +46,8 @@
     a_recv,
     b_send,
     b_recv,
+    relay,
+    relay_recv,
 ):
     levels, rows, depth = spikes_ref.shape
     columns = right_ref.shape[1]
@@ -106,18 +108,18 @@
     for level in range(levels):
         group, offset, base, is_left, relative, holder = position(level)
 
-        @pl.when((offset == max(group - 2, 0)) & (node >= half_nodes))
+        @pl.when(offset == max(group - 2, 0))
         def _():
             greet(place(base + group, node))
 
-        expected += count((offset == group) & (node >= half_nodes))
+        expected += count(offset == group)
         bit = group // 2
         while bit >= 1:
-            @pl.when(holder & (lax.rem(relative, 2 * bit) == bit))
+            @pl.when(lax.rem(relative, 2 * bit) == bit)
             def _(bit=bit):
                 greet(place(tree_dom(group, base, is_left, relative - bit), node))
 
-            expected += count(holder & (lax.rem(relative, 2 * bit) == 0))
+            expected += count(lax.rem(relative, 2 * bit) == 0)
             bit //= 2
     pl.semaphore_wait(barrier, expected)
 
@@ -214,7 +216,10 @@
         @pl.when(from_bottom)
         def _():
             for c in range(PARTS):
-                send_tips(cur.at[level], 0, 2 * nodes * level, c, place(dom + 1, nodes - 1))
+                first = nodes - 1
+                send_tips(
+                    cur.at[level], 0, 2 * nodes * (levels + c % 2) + level, c, place(dom + 1, first)
+                )
 
         def across(step):
             return lax.rem(node + step, nodes)
@@ -234,50 +239,57 @@
 
         piece_at = lax.rem(node, half_nodes)
 
-        def spread(source, c, wait):
-            def go(copy):
-                copy.wait_send() if wait else copy.start()
-
-            cut = piece_cut[c]
-            target = halves.at[level, pl.ds(piece_at * inv_rows + c * piece_chunk, piece_chunk)]
-            if wait:
-                source, target = source, halves.at[level, pl.ds(piece_at * inv_rows, inv_rows)]
-            else:
-                source = source.at[cut]
-            recv = b_recv.at[level, piece_at, c]
+        def slot(c):
+            return halves.at[level, pl.ds(piece_at * inv_rows + c * piece_chunk, piece_chunk)]
+
+        def some(share):
+            return halves.at[level, pl.ds(0, inv_rows // share)]
+
+        def down(source, c, share=0):
             bit, number = group // 2, 0
             while bit >= 1:
-                child = relative + bit
-                child_dom = tree_dom(group, base, is_left, child)
 
                 @pl.when(lax.rem(relative, 2 * bit) == 0)
-                def _(number=number, child_dom=child_dom):
-                    go(copy_to(source, target, b_send.at[level, number], recv, place(child_dom, node)))
+                def _(number=number, bit=bit):
+                    where = place(tree_dom(group, base, is_left, relative + bit), node)
+                    sem = b_send.at[level, number]
+                    if share:
+                        copy_to(some(share), some(share), sem, b_recv.at[level, 0, 0], where).wait_send()
+                    else:
+                        recv = b_recv.at[level, piece_at, c]
+                        copy_to(source.at[piece_cut[c]], slot(c), sem, recv, where).start()
 
                 bit //= 2
                 number += 1
+
+        def aside(source, c, share=0):
             for step in range(1, nodes):
-                go(
-                    copy_to(
-                        source,
-                        target,
-                        b_send.at[level, levels + step],
-                        recv,
-                        place(dom, across(step)),
-                    )
-                )
-
-        def to_left(c, wait):
-            whole = pl.ds(piece_at * inv_rows, inv_rows)
-            part = pl.ds(piece_at * inv_rows + c * piece_chunk, piece_chunk)
-            copy = copy_to(
-                piece if wait else piece.at[piece_cut[c]],
-                halves.at[level, whole if wait else part],
-                b_send.at[level, levels],
-                b_recv.at[level, piece_at, c],
-                place(base + entry, node),
-            )
-            copy.wait_send() if wait else copy.start()
+                where = place(dom, across(step))
+                sem = b_send.at[level, levels + 1 + step]
+                if share:
+                    copy_to(some(share), some(share), sem, b_recv.at[level, 0, 0], where).wait_send()
+                else:
+                    recv = b_recv.at[level, piece_at, c]
+                    copy_to(source.at[piece_cut[c]], slot(c), sem, recv, where).start()
+
+        def to_left(c, share=0):
+            where = place(base + entry, node)
+            sem = b_send.at[level, levels + c % 2]
+            if share:
+                copy_to(some(share), some(share), sem, b_recv.at[level, 0, 0], where).wait_send()
+            else:
+                recv = b_recv.at[level, piece_at, c]
+                source = piece if c % 2 == 0 else relay
+                copy_to(source.at[piece_cut[c]], slot(c), sem, recv, where).start()
+
+        def to_relay(c, share=0):
+            where = place(dom, piece_at)
+            sem = b_send.at[level, levels + 1]
+            if share:
+                copy_to(some(share), some(share), sem, relay_recv.at[0], where).wait_send()
+            else:
+                cut = piece_cut[c]
+                copy_to(piece.at[cut], relay.at[cut], sem, relay_recv.at[c], where).start()
 
         @pl.when(is_solver)
         def _():
@@ -286,9 +298,13 @@
 
                 @pl.when(node == nodes - 1)
                 def _():
-                    for step in range(nodes - 1):
+                    for step in range(1, nodes):
                         send_tips(
-                            tips.at[0], 0, 2 * nodes * level + nodes + step, c, place(dom, step)
+                            tips.at[0],
+                            0,
+                            2 * nodes * level + nodes + step,
+                            c,
+                            place(dom, across(step)),
                         )
 
             @pl.when(node == 0)
@@ -305,13 +321,19 @@
             @pl.when(node < half_nodes)
             def _():
                 for c in range(PARTS):
-                    spread(piece, c, False)
+                    if c % 2 == 0:
+                        down(piece, c)
+                    aside(piece, c)
                 halves[level, pl.ds(piece_at * inv_rows, inv_rows)] = piece[...]
+                for c in range(1, PARTS, 2):
+                    part = relay.at[piece_cut[c]]
+                    copy_to(part, part, b_send.at[0, 0], relay_recv.at[c], sibling).wait_recv()
+                    to_left(c)
 
             @pl.when(node >= half_nodes)
             def _():
                 for c in range(PARTS):
-                    to_left(c, False)
+                    to_left(c) if c % 2 == 0 else to_relay(c)
 
         loaded(2 + level)
         for side in range(2):
@@ -330,7 +352,8 @@
         for c in range(PARTS):
             for index in range(half_nodes):
                 mine = is_solver & (node == index)
-                forward = holder & (piece_at == index) & ~mine
+                turn = holder if c % 2 == 0 else ~holder
+                forward = turn & (piece_at == index) & ~mine
 
                 @pl.when(~mine)
                 def _():
@@ -341,42 +364,52 @@
 
                 @pl.when(forward)
                 def _():
-                    spread(halves.at[level, pl.ds(index * inv_rows, inv_rows)], c, False)
+                    source = halves.at[level, pl.ds(index * inv_rows, inv_rows)]
+                    down(source, c)
+
+                    @pl.when(~is_solver)
+                    def _():
+                        aside(source, c)
 
         update = product(spk_hi.at[level], spk_lo.at[level], [(0, halves[level])])
         cur[level + 1] = cur[level] - update
 
         def finish():
+            half_tips = tips.at[0, pl.ds(0, rows // 2)]
+
+            def sent(ref, index):
+                copy_to(ref, ref, a_send.at[index], a_recv.at[0, 0], sibling).wait_send()
+
             @pl.when(from_bottom)
             def _():
-                copy_to(
-                    cur.at[level], tips.at[0], a_send.at[2 * nodes * level], a_recv.at[0, 0],
-                    place(dom + 1, nodes - 1),
-                ).wait_send()
+                for part in range(2):
+                    sent(half_tips, 2 * nodes * (levels + part) + level)
 
             @pl.when(is_solver & (node == 0))
             def _():
                 for step in range(1, nodes):
-                    copy_to(
-                        cur.at[level], tips.at[1], a_send.at[2 * nodes * level + step],
-                        a_recv.at[1, 0], place(dom, step),
-                    ).wait_send()
+                    sent(tips.at[1], 2 * nodes * level + step)
 
             @pl.when(is_solver & (node == nodes - 1))
             def _():
-                for step in range(nodes - 1):
-                    copy_to(
-                        tips.at[0], tips.at[0], a_send.at[2 * nodes * level + nodes + step],
-                        a_recv.at[0, 0], place(dom, step),
-                    ).wait_send()
+                for step in range(1, nodes):
+                    sent(tips.at[0], 2 * nodes * level + nodes + step)
 
             @pl.when(is_solver & (node >= half_nodes))
             def _():
-                to_left(0, True)
-
-            @pl.when(holder)
-            def _():
-                spread(halves.at[level, pl.ds(piece_at * inv_rows, inv_rows)], 0, True)
+                to_left(0, 2)
+                to_relay(1, 2)
+
+            down(piece, 0, 2)
+
+            @pl.when(is_solver & (node < half_nodes))
+            def _():
+                aside(piece, 0, 1)
+                to_left(1, 2)
+
+            @pl.when(~is_solver)
+            def _():
+                aside(piece, 0, 2)
 
         waits.append(finish)
 
@@ -422,10 +455,12 @@
             dma((levels + 2,)),
             dma((levels + 3,)),
             dma((levels + 3,)),
-            dma((2 * nodes * levels,)),
+            dma((2 * nodes * (levels + 2),)),
             dma((2, PARTS)),
-            dma((levels, levels + nodes)),
+            dma((levels, levels + 1 + nodes)),
             dma((levels, nodes // 2, PARTS)),
+            pltpu.VMEM((inv_rows, columns), f32),
+            dma((PARTS,)),
         ],
         compiler_params=pltpu.CompilerParams(
             has_side_effects=True, vmem_limit_bytes=VMEM_LIMIT, collective_id=0

time: 53.5 us -> 102 us (1.91)
  the two profiles are of different devices: /device:TPU:3 before, /device:TPU:7 now
where the time goes in v3:
time: 102 us
  Pallas kernels  100 us (98%)
  local copies, waits for them, and re-layouts  1.57 us (2%)
    pallas_call x1, Pallas kernels, body(): pl.pallas_call(functools.partial(kernel, row_count), out_shape=jax.ShapeD...  100 us

profile of v3, /device:TPU:7, one launch (start us, length us, event | category | flops | bytes accessed | tf_op | source)
XLA Modules:
  0.0 101.8 jit_solution(644852178739398460)
XLA Ops:
  0.0 100.2 %shard_map.37 = f32[256,128]{1,0:T(8,128)} custom-call(f32[256,128]{1,0:T(8,128)} %right_ref.1, f32[3,256,512]{2,1,0:T(8,128)} %spikes_ref.1, f32[1,256,1024]{2,1,0:T(8,128)} %inverse_ref.1), custom_call_target="tpu_custom_call" | custom-call | flops 1207959552 | bytes 2883584 | tf_op jit(solution)/shard_map/pallas_call | solution.py:437
  100.2 1.6 %copy.5 = f32[256,128]{1,0:T(8,128)} copy(f32[256,128]{1,0:T(8,128)} %shard_map.37) | data formatting | bytes 262144
